TPU v7x, 32 devices: a whole 2x2x4 slice. The times are simulated.
32 devices in a mesh: req: 16 (over z, y, core), tp: 2 (over x).
Axes of the slice: x: 2, y: 2, z: 4, core: 2. Of those that a mesh axis runs over, the one named last changes fastest.
Arguments:
- hidden_in: bfloat16 [2048, 5120], P('req', 'tp'), may hold values from -6 to 6
- norm_gain: bfloat16 [5120], P('tp'), may hold values from 0.099609375 to 1.8984375
- q_weight: bfloat16 [5120, 3072], P(None, 'tp'), may hold values from -0.078125 to 0.078125
- q_bias: bfloat16 [3072], P('tp'), may hold values from -4 to 4
- k_weight: bfloat16 [5120, 1024], P(None, 'tp'), may hold values from -0.125 to 0.125
- k_bias: bfloat16 [1024], P('tp'), may hold values from -5 to 5
- v_weight: bfloat16 [5120, 1024], P(None, 'tp'), may hold values from -0.3125 to 0.3125
- v_bias: bfloat16 [1024], P('tp'), may hold values from -10 to 10
- o_weight: bfloat16 [3072, 5120], P('tp'), may hold values from -0.3125 to 0.3125
- prefix_kv: bfloat16 [16384, 2, 1024], P('req', None, 'tp'), as said below
- suffix_len: int32 [16], P('req'), may hold values from 18 to 128, as said below
- req_prefix: int32 [16], P('req'), may hold values from 0 to 3, as said below
- block_owner: int32 [16], replicated, may hold values from 0 to 15, each once
Outputs:
- attn_out: bfloat16 [2048, 5120], P('req', 'tp')
Inputs may be any that keep to these rules, and one draw needn't show every extreme that they name: `suffix_len`: suffix tokens of each request; some request has exactly 128 and some exactly 18. `req_prefix`: every prefix is continued by exactly 4 requests. Block j of prefix p is held by req index block_owner[p * 4 + j]; each req index holds one block. `prefix_kv`: cached keys already carry the rotary embedding of their prefix positions.
All inputs are finite; a program needn't handle non-finite values.
Results may differ from a plain program's by a relative error of at most 0.022.
Values may be sent and summed in bfloat16 or wider, within the bound.
A program may use at most 192 MiB of HBM per device.

v0:
```python
import jax
import jax.numpy as jnp
from jax import lax
from jax.sharding import PartitionSpec as P

HD = 128
NPREF = 4


THETA = 1000000.0
EPSILON = 1e-06


def rotate(heads, positions):
    half = HD // 2
    freqs = THETA ** (-(jnp.arange(half, dtype=jnp.float32) * 2.0) / HD)
    angles = positions.astype(jnp.float32)[:, None] * freqs[None, :]
    cosine = jnp.cos(angles)[:, None, :]
    sine = jnp.sin(angles)[:, None, :]
    first = heads[..., :half]
    second = heads[..., half:]
    return jnp.concatenate(
        [first * cosine - second * sine, second * cosine + first * sine], axis=-1
    )


def block_stats(grouped, keys, values, allowed):
    scores = jnp.einsum(
        "sghd,kgd->sghk", grouped, keys, preferred_element_type=jnp.float32
    ) * HD ** (-0.5)
    if allowed is not None:
        scores = jnp.where(allowed[:, None, None, :], scores, -jnp.inf)
    peak = jnp.max(scores, axis=-1)
    weights = jnp.exp(scores - peak[..., None])
    total = jnp.sum(weights, axis=-1)
    mixed = jnp.einsum(
        "sghk,kgd->sghd", weights.astype(jnp.bfloat16), values, preferred_element_type=jnp.float32
    )
    return (peak, total, mixed)


def combine(first, second):
    peak = jnp.maximum(first[0], second[0])
    left = jnp.exp(first[0] - peak)
    right = jnp.exp(second[0] - peak)
    total = first[1] * left + second[1] * right
    mixed = first[2] * left[..., None] + second[2] * right[..., None]
    return (peak, total, mixed)


def shards(
    hidden_in,
    norm_gain,
    q_weight,
    q_bias,
    k_weight,
    k_bias,
    v_weight,
    v_bias,
    o_weight,
    prefix_kv,
    suffix_len,
    req_prefix,
    block_owner,
):
    length = hidden_in.shape[0]
    devices = lax.axis_size("req")
    owned = devices // NPREF
    block = prefix_kv.shape[0]
    prefix_len = block * owned
    kv_heads = k_weight.shape[1] // HD
    q_heads = q_weight.shape[1] // HD
    group = q_heads // kv_heads
    full, gain = (
        lax.all_gather(hidden_in, "tp", axis=1, tiled=True),
        lax.all_gather(norm_gain, "tp", axis=0, tiled=True),
    )
    tokens = full.astype(jnp.float32)
    meansq = jnp.mean(tokens * tokens, axis=-1, keepdims=True)
    normed = (tokens * lax.rsqrt(meansq + EPSILON) * gain.astype(jnp.float32)).astype(jnp.bfloat16)
    positions = prefix_len + jnp.arange(length, dtype=jnp.int32)
    queries = jnp.dot(normed, q_weight, preferred_element_type=jnp.float32) + q_bias.astype(
        jnp.float32
    )
    queries = rotate(queries.reshape(length, q_heads, HD), positions).astype(jnp.bfloat16)
    queries = queries.reshape(length, kv_heads, group, HD)
    keys = jnp.dot(normed, k_weight, preferred_element_type=jnp.float32) + k_bias.astype(
        jnp.float32
    )
    keys = rotate(keys.reshape(length, kv_heads, HD), positions).astype(jnp.bfloat16)
    values = jnp.dot(normed, v_weight, preferred_element_type=jnp.float32) + v_bias.astype(
        jnp.float32
    )
    values = values.astype(jnp.bfloat16).reshape(length, kv_heads, HD)
    slot_index = jnp.arange(length, dtype=jnp.int32)
    causal = slot_index[None, :] <= slot_index[:, None]
    state = block_stats(queries, keys, values, causal)
    which = req_prefix[0]

    def advance(current, cached):
        return (combine(current, block_stats(queries, cached[:, 0], cached[:, 1], None)), None)

    everything = lax.all_gather(prefix_kv, "req", axis=0, tiled=True)
    stacked = everything.reshape(devices, block, 2, kv_heads, HD)
    owners = lax.dynamic_slice_in_dim(block_owner, which * owned, owned)
    chosen = jnp.take(stacked, owners, axis=0)
    state, unused = lax.scan(advance, state, chosen)
    peak, total, mixed = state
    context = (mixed / total[..., None]).astype(jnp.bfloat16).reshape(length, q_heads * HD)
    partial_value = jnp.dot(context, o_weight, preferred_element_type=jnp.float32)
    summed = lax.psum_scatter(
        partial_value.astype(jnp.bfloat16), "tp", scatter_dimension=1, tiled=True
    ).astype(jnp.float32)
    valid = slot_index < suffix_len[0]
    return jnp.where(valid[:, None], summed, jnp.float32(0.0)).astype(jnp.bfloat16)


def solution(mesh):
    placed = (
        P("req", "tp"),
        P("tp"),
        P(None, "tp"),
        P("tp"),
        P(None, "tp"),
        P("tp"),
        P(None, "tp"),
        P("tp"),
        P("tp", None),
        P("req", None, "tp"),
        P("req"),
        P("req"),
        P(),
    )
    return jax.shard_map(
        shards, mesh=mesh, in_specs=placed, out_specs=P("req", "tp"), check_vma=False
    )
```

profile of v0, /device:TPU:0, one launch (start us, length us, event | category | flops | bytes accessed | tf_op | source)
XLA Modules:
  0.0 392.9 jit_solution(8280623124228980135)
XLA Ops:
  6.5 0.7 all-gather.4.cloned.1.call-update
  7.3 0.7 all-gather.6.cloned.1.call-update
  8.1 0.7 convert_element_type.69
  8.7 0.7 reshape.141
  9.4 5.3 %all-gather = bf16[2,1,2560]{2,1,0:T(2,128)(2,1)S(1)} all-gather(bf16[1,1,2560]{2,1,0:T(2,128)(2,1)S(1)} %reshape.141), channel_id=1, replica_groups=mesh['req'=16,'tp'=2] {'tp'}, dimensions={0}, use_global_device_ids=true | all-gather | bytes 15360 | tf_op jit(solution)/shard_map/all_gather | solution.py:76
  14.7 0.7 convert_element_type.67
  15.8 0.7 convert_element_type.70
  17.2 0.7 compare_and_fusion
  18.0 17.9 %all-gather.4.cloned.1.call-done = bf16[128,5120]{1,0:T(8,128)(2,1)} async-done(((bf16[128,2560]{1,0:T(8,128)(2,1)}), bf16[128,5120]{1,0:T(8,128)(2,1)}) %all-gather.4.cloned.1.call-update) | async-done | bytes 1310736 | tf_op jit(solution)/shard_map/all_gather | solution.py:75
  35.9 1.6 fusion.18
  37.6 8.2 %convolution_add_fusion = f32[128,1536]{1,0:T(8,128)S(1)} fusion(bf16[5120,1536]{1,0:T(8,128)(2,1)} %param.17, f32[1536]{0:T(1024)S(1)} %convert_element_type.69, bf16[128,5120]{1,0:T(8,128)(2,1)} %all-gather.4.cloned.1.call-done, f32[5120]{0:T(1024)S(1)} %bitcast.94, f32[128]{0:T(128)S(1)} %add_rsqrt_fusion), kind=kOutput, calls=%fused_computation.28 | convolution fusion | flops 2016083968 | bytes 17852928 | tf_op jit(solution)/shard_map/dot_general | solution.py:82
  45.8 0.3 copy.67
  46.2 0.2 copy.69
  46.4 0.2 copy.68
  46.7 3.4 convolution_add_fusion.2
  50.2 3.4 fusion.23
  53.7 0.2 pad_maximum_fusion
  53.9 0.2 fusion.35
  54.2 0.4 fusion.36
  54.7 0.3 convolution_bitcast_fusion
  55.0 150.6 %all-gather.6.cloned.1.call-done = bf16[16384,2,512]{2,1,0:T(2,128)(2,1)} async-done(((bf16[1024,2,512]{2,1,0:T(2,128)(2,1)}), bf16[16384,2,512]{2,1,0:T(2,128)(2,1)}) %all-gather.6.cloned.1.call-update) | async-done | bytes 33554448 | tf_op jit(solution)/shard_map/all_gather | solution.py:103
  205.6 52.7 %reshape.148 = bf16[16,1024,2,4,128]{4,3,2,1,0:T(4,128)(2,1)} reshape(bf16[16384,2,512]{2,1,0:T(2,128)(2,1)} %all-gather.6.cloned.1.call-done) | data formatting | bytes 67108864 | tf_op jit(solution)/shard_map/reshape | solution.py:104
  258.3 22.8 %fusion.34 = (bf16[16,512,2,4,128]{4,3,2,1,0:T(4,128)(2,1)}, bf16[16,512,2,4,128]{4,3,2,1,0:T(4,128)(2,1)}) fusion(bf16[16,1024,2,4,128]{4,3,2,1,0:T(4,128)(2,1)} %reshape.148), kind=kLoop, calls=%fused_computation.61 | loop fusion | bytes 67108864 | tf_op jit(solution)/shard_map/jit(_take)/gather | solution.py:106
  281.1 16.2 %copy.90 = bf16[16,512,2,4,128]{4,1,3,2,0:T(8,128)(2,1)} copy(bf16[16,512,2,4,128]{4,3,2,1,0:T(4,128)(2,1)} %get-tuple-element.61) | data formatting | bytes 33554432
  297.3 7.4 %copy.89 = bf16[16,512,2,4,128]{4,1,3,2,0:T(8,128)(2,1)} copy(bf16[16,512,2,4,128]{4,3,2,1,0:T(4,128)(2,1)S(1)} %copy-done) | data formatting | bytes 33554432
  304.7 8.9 %gather_fusion.1 = bf16[4,512,2,4,128]{4,1,3,2,0:T(8,128)(2,1)} fusion(bf16[16,512,2,4,128]{4,1,3,2,0:T(8,128)(2,1)} %copy.90, s32[1024]{0:T(1024)S(1)} %pad_clamp_fusion), kind=kCustom, calls=%fused_computation.1 | custom fusion | bytes 8388624 | tf_op jit(solution)/shard_map/jit(_take)/gather | solution.py:106
  313.6 8.8 %gather_fusion = bf16[4,512,2,4,128]{4,1,3,2,0:T(8,128)(2,1)} fusion(bf16[16,512,2,4,128]{4,1,3,2,0:T(8,128)(2,1)} %copy.89, s32[1024]{0:T(1024)S(1)} %pad_clamp_fusion), kind=kCustom, calls=%fused_computation | custom fusion | bytes 8388624 | tf_op jit(solution)/shard_map/jit(_take)/gather | solution.py:106
  322.4 7.7 %maximum_select_fusion = bf16[4,1024,2,4,128]{4,1,3,2,0:T(8,128)(2,1)} fusion(bf16[4,512,2,4,128]{4,1,3,2,0:T(8,128)(2,1)} %gather_fusion.1, bf16[4,512,2,4,128]{4,1,3,2,0:T(8,128)(2,1)} %gather_fusion, pred[4]{0:T(512)(128)(4,1)S(1)} %get-tuple-element.56), kind=kLoop, calls=%fused_computation.21 | loop fusion | flops 20971520 | bytes 16777220 | tf_op jit(solution)/shard_map/jit(_take)/select_n | solution.py:106
  330.1 21.9 %while.14 = (s32[]{:T(128)}, f32[128,4,3]{0,2,1:T(4,128)S(1)}, f32[128,4,3]{0,2,1:T(4,128)S(1)}, f32[128,4,3,128]{0,3,2,1:T(8,128)S(1)}, bf16[4,1024,2,4,128]{4,...) while((s32[]{:T(128)}, f32[128,4,3]{0,2,1:T(4,128)S(1)}, f32[128,4,3]{0,2,1:T(4,128)S(1)}, ...), condition=%wide.region_6.7_spmd, body=%wide.region_3.0_spmd.sunk | while | flops 818485248 | bytes 27224152 | solution.py:107
  330.1 1.7 dynamic-slice_bitcast_fusion.2
  331.9 1.0 bitcast_reduce_fusion.2
  332.9 1.0 fusion.51
  333.9 1.6 fusion.52
  335.6 1.7 dynamic-slice_bitcast_fusion.2
  337.3 1.0 bitcast_reduce_fusion.2
  338.3 1.0 fusion.51
  339.4 1.6 fusion.52
  341.1 1.7 dynamic-slice_bitcast_fusion.2
  342.8 1.0 bitcast_reduce_fusion.2
  343.8 1.0 fusion.51
  344.9 1.6 fusion.52
  346.5 1.7 dynamic-slice_bitcast_fusion.2
  348.3 1.0 bitcast_reduce_fusion.2
  349.3 1.0 fusion.51
  350.4 1.6 fusion.52
  352.1 8.8 %convolution_convert_fusion = bf16[128,5120]{1,0:T(8,128)(2,1)} fusion(bf16[128,1536]{0,1:T(8,128)(2,1)S(1)} %bitcast.90, bf16[1536,5120]{1,0:T(8,128)(2,1)} %param.23), kind=kOutput, calls=%fused_computation.22 | convolution fusion | flops 2013921280 | bytes 17432576 | tf_op jit(solution)/shard_map/dot_general | solution.py:110
  361.6 22.7 %reduce-scatter.2.cloned.1.call-done = bf16[128,2560]{1,0:T(8,128)(2,1)} async-done(((bf16[128,5120]{1,0:T(8,128)(2,1)}), bf16[128,2560]{1,0:T(8,128)(2,1)}) %reduce-scatter.2.cloned.1.call-update) | async-done | bytes 655376 | tf_op jit(solution)/shard_map/reduce_scatter | solution.py:111
  384.3 2.1 select_convert_fusion
  (28 shorter events, 1.3 us)
Async XLA Ops:
  6.5 29.3 %all-gather.4.cloned.1.call-start = ((), (), s32[]{:S(2)}) async-start(), calls=%async_computation.1 | async-start | bytes 1966080 | tf_op jit(solution)/shard_map/all_gather | solution.py:75
  7.3 198.3 %all-gather.6.cloned.1.call-start = ((), (), s32[]{:S(2)}) async-start(), calls=%async_computation.2 | async-start | bytes 35651584 | tf_op jit(solution)/shard_map/all_gather | solution.py:103
  8.0 376.3 %reduce-scatter.2.cloned.1.call-start = ((), (), s32[]{:S(2)}) async-start(), calls=%async_computation.3 | async-start | bytes 1966080 | tf_op jit(solution)/shard_map/reduce_scatter | solution.py:111
  37.5 9.1 %copy-start.1 = (bf16[128,5120]{1,0:T(8,128)(2,1)S(1)}, bf16[128,5120]{1,0:T(8,128)(2,1)}, u32[]{:S(2)}) copy-start(bf16[128,5120]{1,0:T(8,128)(2,1)} %all-gather.4.cloned.1.call-done) | copy-start | bytes 3932164
  281.1 16.2 %copy-start = (bf16[16,512,2,4,128]{4,3,2,1,0:T(4,128)(2,1)S(1)}, bf16[16,512,2,4,128]{4,3,2,1,0:T(4,128)(2,1)}, u32[]{:S(2)}) copy-start(bf16[16,512,2,4,128]{4,3,2,1,0:T(4,128)(2,1)} %get-tuple-element.60) | copy-start | bytes 50331652
Sparse Core Ops, SparseCore 0:
  8.9 26.9 all-gather.3
  37.5 168.0 all-gather.5
  361.1 23.1 reduce-scatter.1
where the time goes:
time: 395 us; the launch traced here: 393 us
  waiting for transfers between devices  193 us (49%)
  local copies, waits for them, and re-layouts  126 us (32%)
  matrix products  35 us (9%)
  other arithmetic  19.4 us (5%)
  between operations  14.6 us (4%)
  blocking collectives  5.26 us (1%)
    all_gather x1, waiting for transfers between devices, shards(): everything = lax.all_gather(prefix_kv, 'req', axis=0, tiled=True)  151 us
    reshape x1, local copies, waits for them, and re-layouts, shards(): stacked = everything.reshape(devices, block, 2, kv_heads, HD)  52.7 us
    gather x3, local copies, waits for them, and re-layouts, shards(): chosen = jnp.take(stacked, owners, axis=0)  40.5 us
    unnamed x7, local copies, waits for them, and re-layouts  24.3 us
    reduce_scatter x1, waiting for transfers between devices, shards(): lax.psum_scatter(partial_value.astype(jnp.bfloat16), 'tp', scatter_dimens...  22.7 us
    all_gather x1, waiting for transfers between devices, shards(): lax.all_gather(hidden_in, 'tp', axis=1, tiled=True)  17.9 us
    dot_general x1, matrix products, shards(): jnp.dot(context, o_weight, preferred_element_type=jnp.float32)  8.82 us
    dot_general x1, matrix products, shards(): jnp.dot(normed, q_weight, preferred_element_type=jnp.float32)  8.22 us
  transfers between devices with their start and end apart: 3, of which 3 were waited for; matrix products, arithmetic and copies ran while one was open for 6% of the time, Pallas kernels for 0%

commit v1 on v0

v1 whole, which is shorter than its diff:
```python
import functools

import jax
import jax.numpy as jnp
import numpy as np
from jax import lax
from jax.experimental import pallas as pl
from jax.experimental.pallas import tpu as pltpu
from jax.sharding import PartitionSpec as P

HD = 128
NPREF = 4
OUTER = 4
PAD = 8

THETA = 1000000.0
EPSILON = 1e-06
LOWEST = -1e30
MIB = 1024 * 1024
MESH = pl.DeviceIdType.MESH
NT = (((1,), (1,)), ((), ()))


def flip(index, mask):
    bit = 1
    while bit <= mask:
        if mask & bit:
            index = index + bit - 2 * bit * lax.rem(lax.div(index, bit), 2)
        bit *= 2
    return index


def tables(positions):
    freqs = np.float32(THETA) ** (-(np.arange(HD // 2, dtype=np.float32) * 2.0) / HD)
    angles = positions.astype(np.float32)[:, None] * freqs.astype(np.float32)[None, :]
    cosine = np.cos(angles.astype(np.float64)).astype(np.float32)
    sine = np.sin(angles.astype(np.float64)).astype(np.float32)
    return np.concatenate([cosine, cosine], 1), np.concatenate([-sine, sine], 1)


def greet(req, tp, req_masks, tp_masks):
    barrier = pltpu.get_barrier_semaphore()
    for mask in req_masks:
        pl.semaphore_signal(barrier, inc=1, device_id=(flip(req, mask), tp), device_id_type=MESH)
    for mask in tp_masks:
        pl.semaphore_signal(barrier, inc=1, device_id=(req, flip(tp, mask)), device_id_type=MESH)
    pl.semaphore_wait(barrier, len(req_masks) + len(tp_masks))


def to_row(columns, length):
    lane = lax.broadcasted_iota(jnp.int32, (length, length), 1)
    square = jnp.zeros((length, length), jnp.float32)
    for n, column in enumerate(columns):
        square = jnp.where(lane == n, column, square)
    return jnp.transpose(square)[:PAD]


def project_kernel(
    cfg, hidden, gain, bias, cosine, sine, kvs, wq, wk, wv,
    qg, kvg, own_out, own_lse,
    xbuf, gbuf, normed, vq, vk, vv, qbuf,
    wsem, lsem, xsend, xrecv, gsend, grecv, qsend, qrecv, ksend, krecv,
):
    tps, inner, split, slots, kv_heads, group = cfg
    length, width = hidden.shape
    half = kv_heads // split
    req, tp = lax.axis_index("req"), lax.axis_index("tp")
    part = lax.rem(req, split)

    loads = [
        pltpu.make_async_copy(src, dst, wsem.at[n])
        for n, (src, dst) in enumerate(((wq, vq), (wk, vk), (wv, vv)))
    ]
    for load in loads:
        load.start()
    greet(req, tp, sorted(set(slots[1:]) | set(range(1, inner))), range(1, tps))

    swaps = []
    for k in range(1, tps):
        for src, dst, send, recv in ((hidden, xbuf, xsend, xrecv), (gain, gbuf, gsend, grecv)):
            swaps.append(
                pltpu.make_async_remote_copy(
                    src_ref=src,
                    dst_ref=dst.at[tp],
                    send_sem=send.at[k - 1],
                    recv_sem=recv.at[k - 1],
                    device_id=(req, flip(tp, k)),
                    device_id_type=MESH,
                )
            )
    for swap in swaps:
        swap.start()
    blocks = []
    for k in range(inner - 1, 0, -1):
        blocks.append(
            pltpu.make_async_remote_copy(
                src_ref=kvs.at[lax.rem(flip(req, k), split)],
                dst_ref=kvg.at[k],
                send_sem=ksend.at[k - 1],
                recv_sem=krecv.at[k - 1],
                device_id=(flip(req, k), tp),
                device_id_type=MESH,
            )
        )
    for copy in blocks:
        copy.start()
    keep = pltpu.make_async_copy(kvs.at[part], kvg.at[0], lsem.at[0])
    keep.start()
    xbuf[tp] = hidden[...]
    gbuf[tp] = gain[...]
    for swap in swaps:
        swap.wait()

    square = jnp.zeros((length, 1), jnp.float32)
    for t in range(tps):
        tokens = xbuf[t].astype(jnp.float32)
        square = square + jnp.sum(tokens * tokens, axis=1, keepdims=True)
    factor = lax.rsqrt(square / (tps * width) + EPSILON)
    for t in range(tps):
        tokens = xbuf[t].astype(jnp.float32) * factor * gbuf[t][:1]
        normed[:, t * width : (t + 1) * width] = tokens.astype(jnp.bfloat16)

    def rope(x):
        return x * cosine[...] + pltpu.roll(x, HD // 2, 1) * sine[...]

    for load in loads:
        load.wait()
    span = group * HD
    for g in range(kv_heads):
        q = jnp.dot(
            normed[...], vq[:, g * span : (g + 1) * span], preferred_element_type=jnp.float32
        )
        q = q + bias[:, g * span : (g + 1) * span]
        for h in range(group):
            qbuf[g // half, g % half, h * length : (h + 1) * length] = rope(
                q[:, h * HD : (h + 1) * HD]
            ).astype(jnp.bfloat16)
    asks = []
    for n, mask in enumerate(slots[1:]):
        asks.append(
            pltpu.make_async_remote_copy(
                src_ref=qbuf.at[lax.rem(flip(req, mask), split)],
                dst_ref=qg.at[n + 1],
                send_sem=qsend.at[n],
                recv_sem=qrecv.at[n],
                device_id=(flip(req, mask), tp),
                device_id_type=MESH,
            )
        )
    for ask in asks:
        ask.start()
    mine = pltpu.make_async_copy(qbuf.at[part], qg.at[0], lsem.at[1])
    mine.start()

    first = kv_heads * span
    rows = group * length
    slot = lax.rem(lax.broadcasted_iota(jnp.int32, (rows, length), 0), length)
    allowed = lax.broadcasted_iota(jnp.int32, (rows, length), 1) <= slot
    k_all = jnp.dot(normed[...], vk[...], preferred_element_type=jnp.float32)
    k_all = k_all + bias[:, first : first + kv_heads * HD]
    first += kv_heads * HD
    v_all = jnp.dot(normed[...], vv[...], preferred_element_type=jnp.float32)
    v_all = (v_all + bias[:, first : first + kv_heads * HD]).astype(jnp.bfloat16)
    for p in range(split):
        columns = []
        for g in range(half):
            at = (p * half + g) * HD
            keys = rope(k_all[:, at : at + HD]).astype(jnp.bfloat16)
            scores = lax.dot_general(qbuf[p, g], keys, NT, preferred_element_type=jnp.float32)
            scores = jnp.where(allowed, scores * HD ** (-0.5), -jnp.inf)
            top = jnp.max(scores, axis=1, keepdims=True)
            weights = jnp.exp(scores - top)
            total = jnp.sum(weights, axis=1, keepdims=True)
            out = jnp.dot(
                weights.astype(jnp.bfloat16),
                v_all[:, at : at + HD],
                preferred_element_type=jnp.float32,
            )
            own_out[p, g] = (out / total).astype(jnp.bfloat16)
            column = top + jnp.log(total)
            columns += [column[h * length : (h + 1) * length] for h in range(group)]
        own_lse[p] = to_row(columns, length)

    keep.wait()
    mine.wait()
    for copy in asks + blocks:
        copy.wait()


def project(hidden, gain, bias, cosine, sine, kvs, wq, wk, wv, cfg):
    tps, inner, split, slots, kv_heads, group = cfg
    length, width = hidden.shape
    half = kv_heads // split
    rows = group * length
    vmem = pl.BlockSpec(memory_space=pltpu.VMEM)
    hbm = pl.BlockSpec(memory_space=pl.ANY)
    bf16, f32 = jnp.bfloat16, jnp.float32
    dma = pltpu.SemaphoreType.DMA
    return pl.pallas_call(
        functools.partial(project_kernel, cfg),
        in_specs=[vmem] * 5 + [hbm] * 4,
        out_specs=[hbm, hbm, vmem, vmem],
        out_shape=[
            jax.ShapeDtypeStruct((len(slots), half, rows, HD), bf16),
            jax.ShapeDtypeStruct((inner,) + kvs.shape[1:], bf16),
            jax.ShapeDtypeStruct((split, half, rows, HD), bf16),
            jax.ShapeDtypeStruct((split, PAD, length), f32),
        ],
        scratch_shapes=[
            pltpu.VMEM((tps, length, width), bf16),
            pltpu.VMEM((tps,) + gain.shape, f32),
            pltpu.VMEM((length, tps * width), bf16),
            pltpu.VMEM(wq.shape, bf16),
            pltpu.VMEM(wk.shape, bf16),
            pltpu.VMEM(wv.shape, bf16),
            pltpu.VMEM((split, half, rows, HD), bf16),
            dma((3,)),
            dma((2,)),
            dma((tps - 1,)),
            dma((tps - 1,)),
            dma((tps - 1,)),
            dma((tps - 1,)),
            dma((len(slots) - 1,)),
            dma((len(slots) - 1,)),
            dma((inner - 1,)),
            dma((inner - 1,)),
        ],
        compiler_params=pltpu.CompilerParams(
            collective_id=0, has_side_effects=True, vmem_limit_bytes=52 * MIB
        ),
        name="project",
    )(hidden, gain, bias, cosine, sine, kvs, wq, wk, wv)


def attend_kernel(group, flags, qs, ks, vs, out, lse, acc, peak, total):
    slots, _, rows, _ = qs.shape
    inner = ks.shape[0]
    length = rows // group
    scale = HD ** (-0.5)
    head = pl.program_id(0)
    peak[...] = jnp.full_like(peak, LOWEST)
    total[...] = jnp.zeros_like(total)
    acc[...] = jnp.zeros_like(acc)

    @pl.loop(0, slots * inner)
    def _(pair):
        @pl.when(flags[pair] == 1)
        def _():
            s, k = lax.div(pair, inner), lax.rem(pair, inner)
            scores = (
                lax.dot_general(qs[s, 0], ks[k], NT, preferred_element_type=jnp.float32) * scale
            )
            old = peak[s]
            top = jnp.maximum(old, jnp.max(scores, axis=1, keepdims=True))
            weights = jnp.exp(scores - top)
            fade = jnp.exp(old - top)
            peak[s] = top
            total[s] = total[s] * fade + jnp.sum(weights, axis=1, keepdims=True)
            acc[s] = acc[s] * fade + jnp.dot(
                weights.astype(jnp.bfloat16), vs[k], preferred_element_type=jnp.float32
            )

    row = lax.broadcasted_iota(jnp.int32, (PAD, length), 0)

    @pl.loop(0, slots)
    def _(s):
        whole = total[s]
        some = whole > 0.0
        safe = jnp.where(some, whole, 1.0)
        out[s, 0] = (acc[s] / safe).astype(jnp.bfloat16)
        column = jnp.where(some, peak[s] + jnp.log(safe), LOWEST)
        lse[s, 0] = to_row([column[h * length : (h + 1) * length] for h in range(group)], length)


def attend(flags, qg, kvg, group):
    slots, heads, rows, _ = qg.shape
    inner, block, _ = kvg.shape
    length = rows // group
    return pl.pallas_call(
        functools.partial(attend_kernel, group),
        grid_spec=pltpu.PrefetchScalarGridSpec(
            num_scalar_prefetch=1,
            grid=(heads,),
            in_specs=[
                pl.BlockSpec((slots, 1, rows, HD), lambda g, f: (0, g, 0, 0)),
                pl.BlockSpec((inner, block, HD), lambda g, f: (0, 0, g)),
                pl.BlockSpec((inner, block, HD), lambda g, f: (0, 0, heads + g)),
            ],
            out_specs=[
                pl.BlockSpec((slots, 1, rows, HD), lambda g, f: (0, g, 0, 0)),
                pl.BlockSpec((slots, 1, PAD, length), lambda g, f: (0, g, 0, 0)),
            ],
            scratch_shapes=[
                pltpu.VMEM((slots, rows, HD), jnp.float32),
                pltpu.VMEM((slots, rows, 1), jnp.float32),
                pltpu.VMEM((slots, rows, 1), jnp.float32),
            ],
        ),
        out_shape=[
            jax.ShapeDtypeStruct((slots, heads, rows, HD), jnp.bfloat16),
            jax.ShapeDtypeStruct((slots, heads, PAD, length), jnp.float32),
        ],
        compiler_params=pltpu.CompilerParams(vmem_limit_bytes=48 * MIB),
        name="attend",
    )(flags, qg, kvg, kvg)


def finish_kernel(
    cfg, outs, lses, own_out, own_lse, wo,
    result,
    obuf, lbuf, vo, square, context, psend, precv,
    wsem, lsem, osend, orecv, ssend, srecv, xsend, xrecv,
):
    tps, inner, split, slots, kv_heads, group = cfg
    half = kv_heads // split
    length, width = result.shape
    tile = 512 if width % 512 == 0 else width
    req, tp = lax.axis_index("req"), lax.axis_index("tp")
    part = lax.rem(req, split)

    load = pltpu.make_async_copy(wo, vo, wsem.at[0])
    load.start()
    greet(req, tp, slots[1:], range(1, tps))
    copies = []
    for n in range(len(slots) - 1, 0, -1):
        for src, dst, send, recv in ((lses, lbuf, ssend, srecv), (outs, obuf, osend, orecv)):
            copies.append(
                pltpu.make_async_remote_copy(
                    src_ref=src.at[n],
                    dst_ref=dst.at[n],
                    send_sem=send.at[n - 1],
                    recv_sem=recv.at[n - 1],
                    device_id=(flip(req, slots[n]), tp),
                    device_id_type=MESH,
                )
            )
    for copy in copies:
        copy.start()
    keeps = [
        pltpu.make_async_copy(outs.at[0], obuf.at[0], lsem.at[0]),
        pltpu.make_async_copy(lses.at[0], lbuf.at[0], lsem.at[1]),
    ]
    for keep in keeps:
        keep.start()
    for copy in keeps + copies:
        copy.wait()

    square[...] = jnp.zeros_like(square)
    terms = OUTER + 1
    for sub in range(split):
        which = flip(part, sub)
        for g in range(half):
            parts = [lbuf[so * split + sub, g] for so in range(OUTER)]
            own = own_lse[which]
            parts.append(own[g * group : (g + 1) * group])
            parts = [p[:group] for p in parts]
            top = functools.reduce(jnp.maximum, parts)
            shares = [jnp.exp(p - top) for p in parts]
            whole = functools.reduce(jnp.add, shares)
            for j, share in enumerate(shares):
                at = ((sub * half + g) * terms + j) * group
                square[at : at + group] = share / whole
    columns = jnp.transpose(square[...])
    for sub in range(split):
        which = flip(part, sub)
        for g in range(half):
            for h in range(group):
                total = jnp.zeros((length, HD), jnp.float32)
                for j in range(terms):
                    at = ((sub * half + g) * terms + j) * group + h
                    rows = slice(h * length, (h + 1) * length)
                    if j < OUTER:
                        piece = obuf[j * split + sub, g, rows]
                    else:
                        piece = own_out[which, g, rows]
                    total = total + piece.astype(jnp.float32) * columns[:, at : at + 1]
                to = pl.multiple_of(((which * half + g) * group + h) * HD, HD)
                context[:, pl.ds(to, HD)] = total.astype(jnp.bfloat16)

    load.wait()

    def product(target, n):
        at = pl.multiple_of(target * width + n * tile, 128)
        return jnp.dot(
            context[...], vo[:, pl.ds(at, tile)], preferred_element_type=jnp.float32
        ).astype(jnp.bfloat16)

    swaps = []
    for k in range(1, tps):
        for n in range(width // tile):
            psend[k - 1, :, n * tile : (n + 1) * tile] = product(flip(tp, k), n)
        swap = pltpu.make_async_remote_copy(
            src_ref=psend.at[k - 1],
            dst_ref=precv.at[k - 1],
            send_sem=xsend.at[k - 1],
            recv_sem=xrecv.at[k - 1],
            device_id=(req, flip(tp, k)),
            device_id_type=MESH,
        )
        swap.start()
        swaps.append(swap)
    for n in range(width // tile):
        result[:, n * tile : (n + 1) * tile] = product(tp, n).astype(jnp.float32)
    for k, swap in enumerate(swaps):
        swap.wait()
        result[...] += precv[k].astype(jnp.float32)


def finish(outs, lses, own_out, own_lse, wo, cfg):
    tps, inner, split, slots, kv_heads, group = cfg
    length = lses.shape[-1]
    width = wo.shape[1] // tps
    vmem = pl.BlockSpec(memory_space=pltpu.VMEM)
    hbm = pl.BlockSpec(memory_space=pl.ANY)
    bf16, f32 = jnp.bfloat16, jnp.float32
    dma = pltpu.SemaphoreType.DMA
    return pl.pallas_call(
        functools.partial(finish_kernel, cfg),
        in_specs=[hbm, hbm, vmem, vmem, hbm],
        out_specs=vmem,
        out_shape=jax.ShapeDtypeStruct((length, width), f32),
        scratch_shapes=[
            pltpu.VMEM(outs.shape, bf16),
            pltpu.VMEM(lses.shape, f32),
            pltpu.VMEM(wo.shape, bf16),
            pltpu.VMEM((128, length), f32),
            pltpu.VMEM((length, wo.shape[0]), bf16),
            pltpu.VMEM((tps - 1, length, width), bf16),
            pltpu.VMEM((tps - 1, length, width), bf16),
            dma((1,)),
            dma((2,)),
            dma((len(slots) - 1,)),
            dma((len(slots) - 1,)),
            dma((len(slots) - 1,)),
            dma((len(slots) - 1,)),
            dma((tps - 1,)),
            dma((tps - 1,)),
        ],
        compiler_params=pltpu.CompilerParams(
            collective_id=1, has_side_effects=True, vmem_limit_bytes=52 * MIB
        ),
        name="finish",
    )(outs, lses, own_out, own_lse, wo)


def shards(
    hidden_in,
    norm_gain,
    q_weight,
    q_bias,
    k_weight,
    k_bias,
    v_weight,
    v_bias,
    o_weight,
    prefix_kv,
    suffix_len,
    req_prefix,
    block_owner,
):
    length = hidden_in.shape[0]
    devices = lax.axis_size("req")
    tps = lax.axis_size("tp")
    owned = devices // NPREF
    block = prefix_kv.shape[0]
    kv_heads = k_weight.shape[1] // HD
    group = q_weight.shape[1] // k_weight.shape[1]
    inner = devices // OUTER
    split = 2 if kv_heads % 2 == 0 else 1
    half = kv_heads // split
    slots = tuple(so * inner + sub for so in range(OUTER) for sub in range(split))
    cfg = (tps, inner, split, slots, kv_heads, group)
    me = lax.axis_index("req")

    prefixes = [req_prefix]
    for mask in slots[1:]:
        prefixes.append(
            lax.ppermute(req_prefix, "req", [(r, r ^ mask) for r in range(devices)])
        )
    prefixes = jnp.concatenate(prefixes)
    index = jnp.arange(devices, dtype=jnp.int32)
    blocks = me // inner * inner + (me % inner ^ jnp.arange(inner, dtype=jnp.int32))
    holds = jnp.sum(
        jnp.where(block_owner[None, :] == blocks[:, None], (index // owned)[None, :], 0), axis=1
    )
    flags = (prefixes[:, None] == holds[None, :]).astype(jnp.int32).reshape(-1)

    span = half * HD
    kvs = prefix_kv.reshape(block, 2, split, span).transpose(2, 0, 1, 3)
    kvs = kvs.reshape(split, block, 2 * span)
    gain = jnp.broadcast_to(norm_gain.astype(jnp.float32)[None, :], (8, norm_gain.shape[0]))
    bias = jnp.concatenate([q_bias, k_bias, v_bias]).astype(jnp.float32)[None, :]
    cosine, sine = tables(block * owned + np.arange(length))
    qg, kvg, own_out, own_lse = project(
        hidden_in, gain, bias, jnp.asarray(cosine), jnp.asarray(sine), kvs,
        q_weight, k_weight, v_weight, cfg,
    )
    outs, lses = attend(flags, qg, kvg, group)
    summed = finish(outs, lses, own_out, own_lse, o_weight, cfg)
    valid = jnp.arange(length, dtype=jnp.int32) < suffix_len[0]
    return jnp.where(valid[:, None], summed, jnp.float32(0.0)).astype(jnp.bfloat16)


def solution(mesh):
    placed = (
        P("req", "tp"),
        P("tp"),
        P(None, "tp"),
        P("tp"),
        P(None, "tp"),
        P("tp"),
        P(None, "tp"),
        P("tp"),
        P("tp", None),
        P("req", None, "tp"),
        P("req"),
        P("req"),
        P(),
    )
    return jax.shard_map(
        shards, mesh=mesh, in_specs=placed, out_specs=P("req", "tp"), check_vma=False
    )
```

time: 395 us -> 170 us (0.43); the launches traced: 393 us -> 173 us
  waiting for transfers between devices: 193 us -> 3.19 us
  Pallas kernels: 0 us -> 144 us
  local copies, waits for them, and re-layouts: 126 us -> 12.8 us
  matrix products: 35 us -> 0 us
  other arithmetic: 19.4 us -> 1.26 us
  between operations: 14.6 us -> 1.61 us
  starting transfers between devices: 0.08 us -> 10 us
  blocking collectives: 5.26 us -> 0 us
    all_gather x2 -> x0, waiting for transfers between devices: 169 us -> none  [the longest x1 151 us: shards(): everything = lax.all_gather(prefix_kv, 'req', axis=0, tiled=True)]
    pallas_call x0 -> x3, Pallas kernels: none -> 144 us  [the longest x1 67.7 us: finish(): pl.pallas_call(functools.partial(finish_kernel, cfg), in_specs=[hbm, hbm,...]
    reshape x3 -> x2, local copies, waits for them, and re-layouts: 52.9 us -> 5.69 us  [the longest x1 3.03 us: shards(): kvs = prefix_kv.reshape(block, 2, split, span).transpose(2, 0, 1, 3)]
    gather x3 -> x0, local copies, waits for them, and re-layouts: 40.5 us -> none  [shards(): chosen = jnp.take(stacked, owners, axis=0)]
    dot_general x14 -> x0, matrix products: 35 us -> none  [the longest x1 8.82 us: shards(): jnp.dot(context, o_weight, preferred_element_type=jnp.float32)]
    reduce_scatter x1 -> x0, waiting for transfers between devices: 22.7 us -> none  [shards(): lax.psum_scatter(partial_value.astype(jnp.bfloat16), 'tp', scatter_dimens...]
    unnamed x7 -> x20, local copies, waits for them, and re-layouts: 24.3 us -> 2.64 us
    ppermute x0 -> x7, starting transfers between devices: none -> 10 us  [shards(): lax.ppermute(req_prefix, 'req', [(r, r ^ mask) for r in range(devices)])]
  transfers between devices with their start and end apart: 3 -> 7, of which waited for: 3 -> 2; matrix products, arithmetic and copies ran while one was open for 6% -> 3% of each run, Pallas kernels for 0% -> 30%
where the time goes in v1:
time: 170 us; the launch traced here: 173 us
  Pallas kernels  144 us (85%)
  local copies, waits for them, and re-layouts  12.8 us (8%)
  starting transfers between devices  10 us (6%)
  waiting for transfers between devices  3.19 us (2%)
    pallas_call x1, Pallas kernels, finish(): pl.pallas_call(functools.partial(finish_kernel, cfg), in_specs=[hbm, hbm,...  67.7 us
    pallas_call x1, Pallas kernels, project(): pl.pallas_call(functools.partial(project_kernel, cfg), in_specs=[vmem] *...  52.4 us
    pallas_call x1, Pallas kernels, attend(): pl.pallas_call(functools.partial(attend_kernel, group), grid_spec=pltpu.P...  24.2 us
    ppermute x7, starting transfers between devices, shards(): lax.ppermute(req_prefix, 'req', [(r, r ^ mask) for r in range(devices)])  10 us
    concatenate x1, local copies, waits for them, and re-layouts, shards(): prefixes = jnp.concatenate(prefixes)  4.37 us
  transfers between devices with their start and end apart: 7, of which 2 were waited for; matrix products, arithmetic and copies ran while one was open for 3% of the time, Pallas kernels for 30%

profile of v1, /device:TPU:0, one launch (start us, length us, event | category | flops | bytes accessed | tf_op | source)
XLA Modules:
  0.0 173.1 jit_solution(15801899510085538176)
XLA Ops:
  0.0 0.5 collective-permute-start
  0.5 2.6 %collective-permute-start.1 = (s32[1]{0:T(128)}, s32[1]{0:T(128)}, u32[]{:S(2)}, u32[]{:S(2)}) collective-permute-start(s32[1]{0:T(128)} %param.26), channel_id=1, source_target_pairs={{0,8},{2,10},{4,12},{6,14},{8,0},{10,2},{12,4},{14,6},{16,24},{18,... | collective-permute-start | bytes 20 | tf_op jit(solution)/shard_map/ppermute | solution.py:478
  3.0 0.1 collective-permute-start.2
  3.2 2.7 %collective-permute-start.3 = (s32[1]{0:T(128)}, s32[1]{0:T(128)}, u32[]{:S(2)}, u32[]{:S(2)}) collective-permute-start(s32[1]{0:T(128)} %param.26), channel_id=1, source_target_pairs={{0,16},{2,18},{4,20},{6,22},{8,24},{10,26},{12,28},{14,30},{16,0},... | collective-permute-start | bytes 20 | tf_op jit(solution)/shard_map/ppermute | solution.py:478
  5.9 0.0 collective-permute-start.4
  6.6 3.0 %copy.21 = bf16[1024,1,2,2,256]{4,3,1,0,2:T(2,128)(2,1)S(1)} copy(bf16[1024,1,2,2,256]{4,3,2,1,0:T(2,128)(2,1)} %bitcast.10) | data formatting | bytes 4194304 | tf_op jit(solution)/shard_map/reshape | solution.py:489
  9.7 0.0 copy-start.6
  9.7 0.0 copy-start.7
  9.7 0.0 copy-start.8
  9.7 0.0 copy-start.9
  9.7 0.0 copy-start.5
  9.7 0.0 copy-start.2
  9.8 0.0 copy-start.3
  9.8 0.0 copy-start.4
  9.8 2.7 %reshape.81.kvs = bf16[2,1024,512]{2,1,0:T(8,128)(2,1)} reshape(bf16[2,1024,2,256]{3,2,1,0:T(2,128)(2,1)S(1)} %bitcast.9) | data formatting | bytes 4194304 | tf_op jit(solution)/shard_map/reshape | solution.py:490
  12.4 0.0 copy-done.6
  12.4 0.0 copy-done.7
  12.5 0.0 copy-done.8
  13.2 0.0 copy-done.9
  13.2 0.2 select_reduce_fusion
  13.4 0.0 copy-done.5
  13.4 0.0 copy-done.2
  13.4 0.0 copy-done.3
  13.4 0.0 copy-done.4
  13.4 52.4 %project.1 = (bf16[8,2,384,128]{3,2,1,0:T(8,128)(2,1)}, bf16[4,1024,512]{2,1,0:T(8,128)(2,1)}, bf16[2,2,384,128]{3,2,1,0:T(8,128)(2,1)S(1)}, f32[2,8,128]{2,1,0:T(8,128)S(1)}) custom-call(bf16[128,2560]{1,0:T(8,128)(2,1)S(1)} %copy-done.2, f32[8,2560]{1,0:T(8,128)S(1)} %broadcast_in_dim.40.gain, f32[1,2560]{1,0:T(1,128)S(1)} %maximum_convert_fusion.bias, ...), custom_call_target="tpu_custom_call" | custom-call | tf_op jit(solution)/shard_map/project/pallas_call | solution.py:199
  65.8 0.0 collective-permute-done
  65.8 2.5 %collective-permute-start.5 = (s32[1]{0:T(128)}, s32[1]{0:T(128)}, u32[]{:S(2)}, u32[]{:S(2)}) collective-permute-start(s32[1]{0:T(128)} %param.26), channel_id=1, source_target_pairs={{0,24},{2,26},{4,28},{6,30},{8,16},{10,18},{12,20},{14,22},{16,8},... | collective-permute-start | bytes 20 | tf_op jit(solution)/shard_map/ppermute | solution.py:478
  68.3 0.0 collective-permute-done.1
  68.3 1.7 collective-permute-start.6
  70.0 0.0 collective-permute-done.2
  70.0 0.0 collective-permute-done.3
  70.0 0.0 collective-permute-done.4
  70.0 1.3 collective-permute-done.5
  71.3 1.8 %collective-permute-done.6 = s32[1]{0:T(128)} collective-permute-done((s32[1]{0:T(128)}, s32[1]{0:T(128)}, u32[]{:S(2)}, u32[]{:S(2)}) %collective-permute-start.6) | collective-permute-done | bytes 36 | tf_op jit(solution)/shard_map/ppermute | solution.py:478
  73.2 4.4 %concatenate.19 = s32[8]{0:T(128)S(1)} concatenate(s32[1]{0:T(128)S(6)} %copy.23, s32[1]{0:T(128)} %collective-permute-done, s32[1]{0:T(128)} %collective-permute-done.1, s32[1]{0:T(128)} %collective-permute-done.2, s32[1]{0:T(128)} %collective-permute-done.3, s32[1]{0:T(128)} %collective-permute-done.4, s32[1]{0:T(128)} %collective-permute-done.5, s32[1]{0:T(128)} %collective-permute-done.6), dimensions={0} | concatenate | bytes 64 | tf_op jit(solution)/shard_map/concatenate | solution.py:480
  77.5 0.1 compare_convert_fusion
  77.6 0.1 reshape.82.flags
  77.7 0.0 copy-start
  77.7 1.4 copy-done
  79.1 24.2 %attend.1 = (bf16[8,2,384,128]{3,2,1,0:T(8,128)(2,1)S(1)}, f32[8,2,8,128]{3,2,1,0:T(8,128)S(1)}) custom-call(s32[32]{0:T(128)S(1)} %reshape.82.flags, bf16[8,2,384,128]{3,2,1,0:T(8,128)(2,1)S(1)} %copy-done, bf16[4,1024,512]{2,1,0:T(8,128)(2,1)} %get-tuple-element.12.ks.vs, bf16[4,1024,512]{2,1,0:T(8,128)(2,1)} %get-tuple-element.12.ks.vs), custom_call_target="tpu_custom_call" | custom-call | tf_op jit(solution)/shard_map/attend/pallas_call | solution.py:279
  103.3 0.0 copy-start.1
  103.3 1.2 copy-done.1
  104.5 67.7 %finish.1 = f32[128,2560]{1,0:T(8,128)S(1)} custom-call(bf16[8,2,384,128]{3,2,1,0:T(8,128)(2,1)} %copy-done.1, f32[8,2,8,128]{3,2,1,0:T(8,128)S(1)} %get-tuple-element.14.lses, bf16[2,2,384,128]{3,2,1,0:T(8,128)(2,1)S(1)} %get-tuple-element.15.own_out, f32[2,8,128]{2,1,0:T(8,128)S(1)} %get-tuple-element.16.own_lse, bf16[1536,5120]{1,0:T(8,128)(2,1)} %wo.1), custom_call_target="tpu_custom_call" | custom-call | tf_op jit(solution)/shard_map/finish/pallas_call | solution.py:417
  172.2 1.0 select_convert_fusion
  (8 shorter events, 0.1 us)
Async XLA Ops:
  0.0 65.8 %collective-permute-start = (s32[1]{0:T(128)}, s32[1]{0:T(128)}, u32[]{:S(2)}, u32[]{:S(2)}) collective-permute-start(s32[1]{0:T(128)} %param.26), channel_id=1, source_target_pairs={{0,2},{2,0},{4,6},{6,4},{8,10},{10,8},{12,14},{14,12},{16,18},{18,... | collective-permute-start | bytes 20 | tf_op jit(solution)/shard_map/ppermute | solution.py:478
  0.5 67.8 %collective-permute-start.1 = (s32[1]{0:T(128)}, s32[1]{0:T(128)}, u32[]{:S(2)}, u32[]{:S(2)}) collective-permute-start(s32[1]{0:T(128)} %param.26), channel_id=1, source_target_pairs={{0,8},{2,10},{4,12},{6,14},{8,0},{10,2},{12,4},{14,6},{16,24},{18,... | collective-permute-start | bytes 20 | tf_op jit(solution)/shard_map/ppermute | solution.py:478
  3.0 66.9 %collective-permute-start.2 = (s32[1]{0:T(128)}, s32[1]{0:T(128)}, u32[]{:S(2)}, u32[]{:S(2)}) collective-permute-start(s32[1]{0:T(128)} %param.26), channel_id=1, source_target_pairs={{0,10},{2,8},{4,14},{6,12},{8,2},{10,0},{12,6},{14,4},{16,26},{18,... | collective-permute-start | bytes 20 | tf_op jit(solution)/shard_map/ppermute | solution.py:478
  3.2 66.8 %collective-permute-start.3 = (s32[1]{0:T(128)}, s32[1]{0:T(128)}, u32[]{:S(2)}, u32[]{:S(2)}) collective-permute-start(s32[1]{0:T(128)} %param.26), channel_id=1, source_target_pairs={{0,16},{2,18},{4,20},{6,22},{8,24},{10,26},{12,28},{14,30},{16,0},... | collective-permute-start | bytes 20 | tf_op jit(solution)/shard_map/ppermute | solution.py:478
  5.9 64.1 %collective-permute-start.4 = (s32[1]{0:T(128)}, s32[1]{0:T(128)}, u32[]{:S(2)}, u32[]{:S(2)}) collective-permute-start(s32[1]{0:T(128)} %param.26), channel_id=1, source_target_pairs={{0,18},{2,16},{4,22},{6,20},{8,26},{10,24},{12,30},{14,28},{16,2},... | collective-permute-start | bytes 20 | tf_op jit(solution)/shard_map/ppermute | solution.py:478
  9.7 2.8 %copy-start.6 = (bf16[1536]{0:T(1024)(128)(2,1)S(1)}, bf16[1536]{0:T(1024)(128)(2,1)}, u32[]{:S(2)}) copy-start(bf16[1536]{0:T(1024)(128)(2,1)} %param.18) | copy-start | bytes 9220
  9.7 2.8 %copy-start.7 = (bf16[512]{0:T(512)(128)(2,1)S(1)}, bf16[512]{0:T(512)(128)(2,1)}, u32[]{:S(2)}) copy-start(bf16[512]{0:T(512)(128)(2,1)} %param.20) | copy-start | bytes 3076
  9.7 2.8 %copy-start.8 = (bf16[512]{0:T(512)(128)(2,1)S(1)}, bf16[512]{0:T(512)(128)(2,1)}, u32[]{:S(2)}) copy-start(bf16[512]{0:T(512)(128)(2,1)} %param.22) | copy-start | bytes 3076
  9.7 3.5 %copy-start.9 = (s32[16]{0:T(128)S(1)}, s32[16]{0:T(128)}, u32[]{:S(2)}) copy-start(s32[16]{0:T(128)} %param.27) | copy-start | bytes 196
  9.7 3.7 %copy-start.5 = (bf16[2560]{0:T(1024)(128)(2,1)S(1)}, bf16[2560]{0:T(1024)(128)(2,1)}, u32[]{:S(2)}) copy-start(bf16[2560]{0:T(1024)(128)(2,1)} %param.16) | copy-start | bytes 15364
  9.7 3.7 %copy-start.2 = (bf16[128,2560]{1,0:T(8,128)(2,1)S(1)}, bf16[128,2560]{1,0:T(8,128)(2,1)}, u32[]{:S(2)}) copy-start(bf16[128,2560]{1,0:T(8,128)(2,1)} %hidden.1) | copy-start | bytes 1966084
  9.8 3.7 %copy-start.3 = (f32[128,128]{1,0:T(8,128)S(1)}, f32[128,128]{1,0:T(8,128)}, u32[]{:S(2)}) copy-start(f32[128,128]{1,0:T(8,128)} %constant.50.clone.cosine) | copy-start | bytes 196612
  9.8 3.7 %copy-start.4 = (f32[128,128]{1,0:T(8,128)S(1)}, f32[128,128]{1,0:T(8,128)}, u32[]{:S(2)}) copy-start(f32[128,128]{1,0:T(8,128)} %constant.51.clone.sine) | copy-start | bytes 196612
  65.8 5.5 %collective-permute-start.5 = (s32[1]{0:T(128)}, s32[1]{0:T(128)}, u32[]{:S(2)}, u32[]{:S(2)}) collective-permute-start(s32[1]{0:T(128)} %param.26), channel_id=1, source_target_pairs={{0,24},{2,26},{4,28},{6,30},{8,16},{10,18},{12,20},{14,22},{16,8},... | collective-permute-start | bytes 20 | tf_op jit(solution)/shard_map/ppermute | solution.py:478
  68.3 4.9 %collective-permute-start.6 = (s32[1]{0:T(128)}, s32[1]{0:T(128)}, u32[]{:S(2)}, u32[]{:S(2)}) collective-permute-start(s32[1]{0:T(128)} %param.26), channel_id=1, source_target_pairs={{0,26},{2,24},{4,30},{6,28},{8,18},{10,16},{12,22},{14,20},{16,10}... | collective-permute-start | bytes 20 | tf_op jit(solution)/shard_map/ppermute | solution.py:478
  77.7 1.4 copy-start
  103.3 1.2 copy-start.1

commit v2 on v1

v2 whole, which is shorter than its diff:
```python
import functools

import jax
import jax.numpy as jnp
import numpy as np
from jax import lax
from jax.experimental import pallas as pl
from jax.experimental.pallas import tpu as pltpu
from jax.sharding import PartitionSpec as P

HD = 128
NPREF = 4
OUTER = 4
PIECES = 2
PAD = 8

THETA = 1000000.0
EPSILON = 1e-06
LOWEST = -1e30
MIB = 1024 * 1024
MESH = pl.DeviceIdType.MESH
NT = (((1,), (1,)), ((), ()))


def flip(index, mask):
    bit = 1
    while bit <= mask:
        if mask & bit:
            index = index + bit - 2 * bit * lax.rem(lax.div(index, bit), 2)
        bit *= 2
    return index


def tables(positions):
    freqs = np.float32(THETA) ** (-(np.arange(HD // 2, dtype=np.float32) * 2.0) / HD)
    angles = positions.astype(np.float32)[:, None] * freqs.astype(np.float32)[None, :]
    cosine = np.cos(angles.astype(np.float64)).astype(np.float32)
    sine = np.sin(angles.astype(np.float64)).astype(np.float32)
    return np.concatenate([cosine, cosine], 1), np.concatenate([-sine, sine], 1)


def heads_of(column, group, length):
    short = length // PIECES
    return [
        jnp.concatenate(
            [column[(p * group + h) * short :][:short] for p in range(PIECES)], axis=0
        )
        for h in range(group)
    ]


def greet(req, tp, req_masks, tp_masks):
    barrier = pltpu.get_barrier_semaphore()
    for mask in req_masks:
        pl.semaphore_signal(barrier, inc=1, device_id=(flip(req, mask), tp), device_id_type=MESH)
    for mask in tp_masks:
        pl.semaphore_signal(barrier, inc=1, device_id=(req, flip(tp, mask)), device_id_type=MESH)
    pl.semaphore_wait(barrier, len(req_masks) + len(tp_masks))


def to_row(columns, length):
    lane = lax.broadcasted_iota(jnp.int32, (length, length), 1)
    square = jnp.zeros((length, length), jnp.float32)
    for n, column in enumerate(columns):
        square = jnp.where(lane == n, column, square)
    return jnp.transpose(square)[:PAD]


def project_kernel(
    cfg, hidden, gain, bias, cosine, sine, prefix, kvs, wq, wk, wv,
    qg, kvg, prefixes, own_out, own_lse,
    xbuf, gbuf, normed, vq, vk, vv, qbuf,
    wsem, lsem, xsend, xrecv, gsend, grecv, qsend, qrecv, ksend, krecv, psend, precv,
):
    tps, inner, split, slots, kv_heads, group = cfg
    length, width = hidden.shape
    half = kv_heads // split
    req, tp = lax.axis_index("req"), lax.axis_index("tp")
    part = lax.rem(req, split)
    short = length // PIECES
    span = group * HD
    step = group * short

    def cached(side, which):
        return pl.multiple_of((side * split + which) * half * HD, HD)

    loads = [
        pltpu.make_async_copy(src, dst, wsem.at[n])
        for n, (src, dst) in enumerate(((wq, vq), (wk, vk), (wv, vv)))
    ]
    for load in loads:
        load.start()
    greet(req, tp, sorted(set(slots[1:]) | set(range(1, inner))), range(1, tps))

    def swap_of(k, piece):
        rows = pl.ds(piece * short, short)
        return pltpu.make_async_remote_copy(
            src_ref=hidden.at[rows],
            dst_ref=xbuf.at[tp, rows],
            send_sem=xsend.at[piece, k - 1],
            recv_sem=xrecv.at[piece, k - 1],
            device_id=(req, flip(tp, k)),
            device_id_type=MESH,
        )

    gains = [
        pltpu.make_async_remote_copy(
            src_ref=gain,
            dst_ref=gbuf.at[tp],
            send_sem=gsend.at[k - 1],
            recv_sem=grecv.at[k - 1],
            device_id=(req, flip(tp, k)),
            device_id_type=MESH,
        )
        for k in range(1, tps)
    ]
    for copy in gains:
        copy.start()
    swaps = [[swap_of(k, piece) for k in range(1, tps)] for piece in range(PIECES)]
    for swap in swaps[0]:
        swap.start()
    blocks = []
    for k in range(inner - 1, 0, -1):
        for side in range(2):
            there = lax.rem(flip(req, k), split)
            blocks.append(
                pltpu.make_async_remote_copy(
                    src_ref=kvs.at[:, pl.ds(cached(side, there), half * HD)],
                    dst_ref=kvg.at[k, :, pl.ds(side * half * HD, half * HD)],
                    send_sem=ksend.at[k - 1, side],
                    recv_sem=krecv.at[k - 1, side],
                    device_id=(flip(req, k), tp),
                    device_id_type=MESH,
                )
            )
    for copy in blocks:
        copy.start()
    for n, mask in enumerate(slots[1:]):
        copy = pltpu.make_async_remote_copy(
            src_ref=prefix,
            dst_ref=prefixes.at[n + 1],
            send_sem=psend.at[n],
            recv_sem=precv.at[n],
            device_id=(flip(req, mask), tp),
            device_id_type=MESH,
        )
        copy.start()
        blocks.append(copy)
    keeps = [pltpu.make_async_copy(prefix, prefixes.at[0], lsem.at[0])]
    for side in range(2):
        keeps.append(
            pltpu.make_async_copy(
                kvs.at[:, pl.ds(cached(side, part), half * HD)],
                kvg.at[0, :, pl.ds(side * half * HD, half * HD)],
                lsem.at[1 + side],
            )
        )
    for keep in keeps:
        keep.start()
    xbuf[tp] = hidden[...]
    gbuf[tp] = gain[...]

    def rope(x, at):
        return x * cosine[at] + pltpu.roll(x, HD // 2, 1) * sine[at]

    asks = []
    for piece in range(PIECES):
        at = slice(piece * short, (piece + 1) * short)
        if piece + 1 < PIECES:
            for swap, later in zip(swaps[piece], swaps[piece + 1]):
                swap.wait_send()
                later.start()
                swap.wait_recv()
        else:
            for swap in swaps[piece]:
                swap.wait()
        if piece == 0:
            for copy in gains:
                copy.wait()
        square = jnp.zeros((short, 1), jnp.float32)
        for t in range(tps):
            tokens = xbuf[t, at].astype(jnp.float32)
            square = square + jnp.sum(tokens * tokens, axis=1, keepdims=True)
        factor = lax.rsqrt(square / (tps * width) + EPSILON)
        for t in range(tps):
            tokens = xbuf[t, at].astype(jnp.float32) * factor * gbuf[t][:1]
            normed[at, t * width : (t + 1) * width] = tokens.astype(jnp.bfloat16)
        if piece == 0:
            loads[0].wait()
        for g in range(kv_heads):
            q = jnp.dot(
                normed[at], vq[:, g * span : (g + 1) * span], preferred_element_type=jnp.float32
            )
            q = q + bias[:, g * span : (g + 1) * span]
            for h in range(group):
                to = piece * step + h * short
                qbuf[g // half, g % half, to : to + short] = rope(
                    q[:, h * HD : (h + 1) * HD], at
                ).astype(jnp.bfloat16)
        rows = pl.ds(piece * step, step)
        for n, mask in enumerate(slots[1:]):
            ask = pltpu.make_async_remote_copy(
                src_ref=qbuf.at[lax.rem(flip(req, mask), split), :, rows],
                dst_ref=qg.at[n + 1, :, rows],
                send_sem=qsend.at[piece, n],
                recv_sem=qrecv.at[piece, n],
                device_id=(flip(req, mask), tp),
                device_id_type=MESH,
            )
            ask.start()
            asks.append(ask)
    mine = pltpu.make_async_copy(qbuf.at[part], qg.at[0], lsem.at[3])
    mine.start()
    for load in loads[1:]:
        load.wait()

    first = kv_heads * span
    rows = group * length
    slot = lax.broadcasted_iota(jnp.int32, (rows, length), 0)
    slot = lax.div(slot, step) * short + lax.rem(slot, short)
    allowed = lax.broadcasted_iota(jnp.int32, (rows, length), 1) <= slot
    k_all = jnp.dot(normed[...], vk[...], preferred_element_type=jnp.float32)
    k_all = k_all + bias[:, first : first + kv_heads * HD]
    first += kv_heads * HD
    v_all = jnp.dot(normed[...], vv[...], preferred_element_type=jnp.float32)
    v_all = (v_all + bias[:, first : first + kv_heads * HD]).astype(jnp.bfloat16)
    for p in range(split):
        columns = []
        for g in range(half):
            at = (p * half + g) * HD
            keys = rope(k_all[:, at : at + HD], slice(None)).astype(jnp.bfloat16)
            scores = lax.dot_general(qbuf[p, g], keys, NT, preferred_element_type=jnp.float32)
            scores = jnp.where(allowed, scores * HD ** (-0.5), -jnp.inf)
            top = jnp.max(scores, axis=1, keepdims=True)
            weights = jnp.exp(scores - top)
            total = jnp.sum(weights, axis=1, keepdims=True)
            out = jnp.dot(
                weights.astype(jnp.bfloat16),
                v_all[:, at : at + HD],
                preferred_element_type=jnp.float32,
            )
            own_out[p, g] = (out / total).astype(jnp.bfloat16)
            column = top + jnp.log(total)
            columns += heads_of(column, group, length)
        own_lse[p] = to_row(columns, length)

    for keep in keeps:
        keep.wait()
    mine.wait()
    for copy in asks + blocks:
        copy.wait()


def project(hidden, gain, bias, cosine, sine, prefix, kvs, wq, wk, wv, cfg):
    tps, inner, split, slots, kv_heads, group = cfg
    length, width = hidden.shape
    half = kv_heads // split
    rows = group * length
    vmem = pl.BlockSpec(memory_space=pltpu.VMEM)
    hbm = pl.BlockSpec(memory_space=pl.ANY)
    bf16, f32 = jnp.bfloat16, jnp.float32
    dma = pltpu.SemaphoreType.DMA
    return pl.pallas_call(
        functools.partial(project_kernel, cfg),
        in_specs=[vmem] * 6 + [hbm] * 4,
        out_specs=[hbm, hbm, hbm, vmem, vmem],
        out_shape=[
            jax.ShapeDtypeStruct((len(slots), half, rows, HD), bf16),
            jax.ShapeDtypeStruct((inner, kvs.shape[0], 2 * half * HD), bf16),
            jax.ShapeDtypeStruct((len(slots),) + prefix.shape, jnp.int32),
            jax.ShapeDtypeStruct((split, half, rows, HD), bf16),
            jax.ShapeDtypeStruct((split, PAD, length), f32),
        ],
        scratch_shapes=[
            pltpu.VMEM((tps, length, width), bf16),
            pltpu.VMEM((tps,) + gain.shape, f32),
            pltpu.VMEM((length, tps * width), bf16),
            pltpu.VMEM(wq.shape, bf16),
            pltpu.VMEM(wk.shape, bf16),
            pltpu.VMEM(wv.shape, bf16),
            pltpu.VMEM((split, half, rows, HD), bf16),
            dma((3,)),
            dma((4,)),
            dma((PIECES, tps - 1)),
            dma((PIECES, tps - 1)),
            dma((tps - 1,)),
            dma((tps - 1,)),
            dma((PIECES, len(slots) - 1)),
            dma((PIECES, len(slots) - 1)),
            dma((inner - 1, 2)),
            dma((inner - 1, 2)),
            dma((len(slots) - 1,)),
            dma((len(slots) - 1,)),
        ],
        compiler_params=pltpu.CompilerParams(
            collective_id=0, has_side_effects=True, vmem_limit_bytes=52 * MIB
        ),
        name="project",
    )(hidden, gain, bias, cosine, sine, prefix, kvs, wq, wk, wv)


def attend_kernel(group, holds, prefixes, qs, ks, vs, out, lse, ones, acc, peak):
    slots, _, rows, _ = qs.shape
    inner, block, _ = ks.shape
    length = rows // group
    scale = HD ** (-0.5)
    base2 = scale * np.log2(np.e)
    peak[...] = jnp.full_like(peak, LOWEST)
    acc[...] = jnp.zeros_like(acc)
    ones[:, :, :HD] = vs[...]
    ones[:, :, HD:] = jnp.ones((inner, block, HD), jnp.bfloat16)

    @pl.loop(0, slots * inner)
    def _(pair):
        s, k = lax.div(pair, inner), lax.rem(pair, inner)

        @pl.when(prefixes[s, 0, 0] == holds[k])
        def _():
            scores = lax.dot_general(qs[s, 0], ks[k], NT, preferred_element_type=jnp.float32)
            old = peak[s]
            top = jnp.maximum(old, jnp.max(scores, axis=1, keepdims=True))
            weights = jnp.exp2((scores - top) * base2)
            fade = jnp.exp2((old - top) * base2)
            peak[s] = top
            acc[s] = acc[s] * fade + jnp.dot(
                weights.astype(jnp.bfloat16), ones[k], preferred_element_type=jnp.float32
            )

    @pl.loop(0, slots)
    def _(s):
        whole = acc[s, :, HD:]
        some = whole > 0.0
        safe = jnp.where(some, whole, 1.0)
        out[s, 0] = (acc[s, :, :HD] / safe).astype(jnp.bfloat16)
        column = jnp.where(some[:, :1], peak[s] * scale + jnp.log(safe[:, :1]), LOWEST)
        lse[s, 0] = to_row(heads_of(column, group, length), length)


def attend(holds, prefixes, qg, kvg, group):
    slots, heads, rows, _ = qg.shape
    inner, block, _ = kvg.shape
    length = rows // group
    return pl.pallas_call(
        functools.partial(attend_kernel, group),
        grid=(heads,),
        in_specs=[
            pl.BlockSpec(memory_space=pltpu.SMEM),
            pl.BlockSpec(memory_space=pltpu.SMEM),
            pl.BlockSpec((slots, 1, rows, HD), lambda g: (0, g, 0, 0)),
            pl.BlockSpec((inner, block, HD), lambda g: (0, 0, g)),
            pl.BlockSpec((inner, block, HD), lambda g: (0, 0, heads + g)),
        ],
        out_specs=[
            pl.BlockSpec((slots, 1, rows, HD), lambda g: (0, g, 0, 0)),
            pl.BlockSpec((slots, 1, PAD, length), lambda g: (0, g, 0, 0)),
        ],
        scratch_shapes=[
            pltpu.VMEM((inner, block, 2 * HD), jnp.bfloat16),
            pltpu.VMEM((slots, rows, 2 * HD), jnp.float32),
            pltpu.VMEM((slots, rows, 1), jnp.float32),
        ],
        out_shape=[
            jax.ShapeDtypeStruct((slots, heads, rows, HD), jnp.bfloat16),
            jax.ShapeDtypeStruct((slots, heads, PAD, length), jnp.float32),
        ],
        compiler_params=pltpu.CompilerParams(vmem_limit_bytes=48 * MIB),
        name="attend",
    )(holds, prefixes, qg, kvg, kvg)


def finish_kernel(
    cfg, outs, lses, own_out, own_lse, wo,
    result,
    obuf, lbuf, vo, square, context, psend, precv,
    wsem, lsem, osend, orecv, ssend, srecv, xsend, xrecv,
):
    tps, inner, split, slots, kv_heads, group = cfg
    half = kv_heads // split
    length, width = result.shape
    tile = 512 if width % 512 == 0 else width
    req, tp = lax.axis_index("req"), lax.axis_index("tp")
    part = lax.rem(req, split)

    load = pltpu.make_async_copy(wo, vo, wsem.at[0])
    load.start()
    greet(req, tp, slots[1:], range(1, tps))
    short = length // PIECES
    step = group * short
    order = range(len(slots) - 1, 0, -1)
    stats = [
        pltpu.make_async_remote_copy(
            src_ref=lses.at[n],
            dst_ref=lbuf.at[n],
            send_sem=ssend.at[n - 1],
            recv_sem=srecv.at[n - 1],
            device_id=(flip(req, slots[n]), tp),
            device_id_type=MESH,
        )
        for n in order
    ]

    def answer_of(n, piece):
        rows = pl.ds(piece * step, step)
        return pltpu.make_async_remote_copy(
            src_ref=outs.at[n, :, rows],
            dst_ref=obuf.at[n, :, rows],
            send_sem=osend.at[piece, n - 1],
            recv_sem=orecv.at[piece, n - 1],
            device_id=(flip(req, slots[n]), tp),
            device_id_type=MESH,
        )

    answers = [[answer_of(n, piece) for n in order] for piece in range(PIECES)]
    for copy in stats + answers[0]:
        copy.start()
    keeps = [
        pltpu.make_async_copy(outs.at[0], obuf.at[0], lsem.at[0]),
        pltpu.make_async_copy(lses.at[0], lbuf.at[0], lsem.at[1]),
    ]
    for keep in keeps:
        keep.start()
    for copy in keeps + stats:
        copy.wait()

    square[...] = jnp.zeros_like(square)
    terms = OUTER + 1
    for sub in range(split):
        which = flip(part, sub)
        for g in range(half):
            parts = [lbuf[so * split + sub, g] for so in range(OUTER)]
            own = own_lse[which]
            parts.append(own[g * group : (g + 1) * group])
            parts = [p[:group] for p in parts]
            top = functools.reduce(jnp.maximum, parts)
            shares = [jnp.exp(p - top) for p in parts]
            whole = functools.reduce(jnp.add, shares)
            for j, share in enumerate(shares):
                at = ((sub * half + g) * terms + j) * group
                square[at : at + group] = share / whole
    columns = jnp.transpose(square[...])
    def product(target, piece, n):
        at = pl.multiple_of(target * width + n * tile, 128)
        return jnp.dot(
            context[piece * short : (piece + 1) * short],
            vo[:, pl.ds(at, tile)],
            preferred_element_type=jnp.float32,
        ).astype(jnp.bfloat16)

    swaps = []
    for piece in range(PIECES):
        slot_rows = slice(piece * short, (piece + 1) * short)
        if piece + 1 < PIECES:
            for copy, later in zip(answers[piece], answers[piece + 1]):
                copy.wait_send()
                later.start()
            for copy in answers[piece]:
                copy.wait_recv()
        else:
            for copy in answers[piece]:
                copy.wait()
        for sub in range(split):
            which = flip(part, sub)
            for g in range(half):
                for h in range(group):
                    total = jnp.zeros((short, HD), jnp.float32)
                    first = piece * step + h * short
                    rows = slice(first, first + short)
                    for j in range(terms):
                        at = ((sub * half + g) * terms + j) * group + h
                        if j < OUTER:
                            term = obuf[j * split + sub, g, rows]
                        else:
                            term = own_out[which, g, rows]
                        total = total + term.astype(jnp.float32) * columns[slot_rows, at : at + 1]
                    to = pl.multiple_of(((which * half + g) * group + h) * HD, HD)
                    context[slot_rows, pl.ds(to, HD)] = total.astype(jnp.bfloat16)
        if piece == 0:
            load.wait()
        for k in range(1, tps):
            for n in range(width // tile):
                psend[k - 1, slot_rows, n * tile : (n + 1) * tile] = product(
                    flip(tp, k), piece, n
                )
            swap = pltpu.make_async_remote_copy(
                src_ref=psend.at[k - 1, pl.ds(piece * short, short)],
                dst_ref=precv.at[k - 1, pl.ds(piece * short, short)],
                send_sem=xsend.at[piece, k - 1],
                recv_sem=xrecv.at[piece, k - 1],
                device_id=(req, flip(tp, k)),
                device_id_type=MESH,
            )
            swap.start()
            swaps.append((k, slot_rows, swap))
        for n in range(width // tile):
            result[slot_rows, n * tile : (n + 1) * tile] = product(tp, piece, n).astype(
                jnp.float32
            )
    for k, slot_rows, swap in swaps:
        swap.wait()
        result[slot_rows] += precv[k - 1, slot_rows].astype(jnp.float32)


def finish(outs, lses, own_out, own_lse, wo, cfg):
    tps, inner, split, slots, kv_heads, group = cfg
    length = lses.shape[-1]
    width = wo.shape[1] // tps
    vmem = pl.BlockSpec(memory_space=pltpu.VMEM)
    hbm = pl.BlockSpec(memory_space=pl.ANY)
    bf16, f32 = jnp.bfloat16, jnp.float32
    dma = pltpu.SemaphoreType.DMA
    return pl.pallas_call(
        functools.partial(finish_kernel, cfg),
        in_specs=[hbm, hbm, vmem, vmem, hbm],
        out_specs=vmem,
        out_shape=jax.ShapeDtypeStruct((length, width), f32),
        scratch_shapes=[
            pltpu.VMEM(outs.shape, bf16),
            pltpu.VMEM(lses.shape, f32),
            pltpu.VMEM(wo.shape, bf16),
            pltpu.VMEM((128, length), f32),
            pltpu.VMEM((length, wo.shape[0]), bf16),
            pltpu.VMEM((tps - 1, length, width), bf16),
            pltpu.VMEM((tps - 1, length, width), bf16),
            dma((1,)),
            dma((2,)),
            dma((PIECES, len(slots) - 1)),
            dma((PIECES, len(slots) - 1)),
            dma((len(slots) - 1,)),
            dma((len(slots) - 1,)),
            dma((PIECES, tps - 1)),
            dma((PIECES, tps - 1)),
        ],
        compiler_params=pltpu.CompilerParams(
            collective_id=1, has_side_effects=True, vmem_limit_bytes=52 * MIB
        ),
        name="finish",
    )(outs, lses, own_out, own_lse, wo)


def shards(
    hidden_in,
    norm_gain,
    q_weight,
    q_bias,
    k_weight,
    k_bias,
    v_weight,
    v_bias,
    o_weight,
    prefix_kv,
    suffix_len,
    req_prefix,
    block_owner,
):
    length = hidden_in.shape[0]
    devices = lax.axis_size("req")
    tps = lax.axis_size("tp")
    owned = devices // NPREF
    block = prefix_kv.shape[0]
    kv_heads = k_weight.shape[1] // HD
    group = q_weight.shape[1] // k_weight.shape[1]
    inner = devices // OUTER
    split = 2 if kv_heads % 2 == 0 else 1
    slots = tuple(so * inner + sub for so in range(OUTER) for sub in range(split))
    cfg = (tps, inner, split, slots, kv_heads, group)
    me = lax.axis_index("req")

    index = jnp.arange(devices, dtype=jnp.int32)
    blocks = me // inner * inner + (me % inner ^ jnp.arange(inner, dtype=jnp.int32))
    holds = jnp.sum(
        jnp.where(block_owner[None, :] == blocks[:, None], (index // owned)[None, :], 0), axis=1
    )
    prefix = jnp.broadcast_to(req_prefix[:, None], (8, 128))
    kvs = prefix_kv.reshape(block, 2 * kv_heads * HD)
    gain = jnp.broadcast_to(norm_gain.astype(jnp.float32)[None, :], (8, norm_gain.shape[0]))
    bias = jnp.concatenate([q_bias, k_bias, v_bias]).astype(jnp.float32)[None, :]
    cosine, sine = tables(block * owned + np.arange(length))
    qg, kvg, prefixes, own_out, own_lse = project(
        hidden_in, gain, bias, jnp.asarray(cosine), jnp.asarray(sine), prefix, kvs,
        q_weight, k_weight, v_weight, cfg,
    )
    outs, lses = attend(holds, prefixes, qg, kvg, group)
    summed = finish(outs, lses, own_out, own_lse, o_weight, cfg)
    valid = jnp.arange(length, dtype=jnp.int32) < suffix_len[0]
    return jnp.where(valid[:, None], summed, jnp.float32(0.0)).astype(jnp.bfloat16)


def solution(mesh):
    placed = (
        P("req", "tp"),
        P("tp"),
        P(None, "tp"),
        P("tp"),
        P(None, "tp"),
        P("tp"),
        P(None, "tp"),
        P("tp"),
        P("tp", None),
        P("req", None, "tp"),
        P("req"),
        P("req"),
        P(),
    )
    return jax.shard_map(
        shards, mesh=mesh, in_specs=placed, out_specs=P("req", "tp"), check_vma=False
    )
```

time: 170 us -> 145 us (0.85); the launches traced: 173 us -> 145 us
  starting transfers between devices: 10 us -> 0 us
  Pallas kernels: 144 us -> 135 us
  local copies, waits for them, and re-layouts: 12.8 us -> 6.17 us
  waiting for transfers between devices: 3.19 us -> 0 us
    pallas_call x1, Pallas kernels: 67.7 us -> 50.9 us  [finish(): pl.pallas_call(functools.partial(finish_kernel, cfg), in_specs=[hbm, hbm,...]
    ppermute x7 -> x0, starting transfers between devices: 10 us -> none  [shards(): lax.ppermute(req_prefix, 'req', [(r, r ^ mask) for r in range(devices)])]
    pallas_call x1, Pallas kernels: 24.2 us -> 30.7 us  [attend(): pl.pallas_call(functools.partial(attend_kernel, group), grid=(heads,), in...]
    reshape x2 -> x0, local copies, waits for them, and re-layouts: 5.69 us -> none  [the longest x1 3.03 us: shards(): kvs = prefix_kv.reshape(block, 2, split, span).transpose(2, 0, 1, 3)]
    concatenate x1 -> x0, local copies, waits for them, and re-layouts: 4.37 us -> none  [shards(): prefixes = jnp.concatenate(prefixes)]
    unnamed x20 -> x19, local copies, waits for them, and re-layouts: 2.64 us -> 6.14 us
    ppermute x7 -> x0, waiting for transfers between devices: 3.19 us -> none  [shards(): lax.ppermute(req_prefix, 'req', [(r, r ^ mask) for r in range(devices)])]
  transfers between devices with their start and end apart: 7 -> 0, of which waited for: 2 -> 0; matrix products, arithmetic and copies ran while one was open for 3% -> 0% of each run, Pallas kernels for 30% -> 0%
where the time goes in v2:
time: 145 us
  Pallas kernels  135 us (93%)
  local copies, waits for them, and re-layouts  6.17 us (4%)
  other arithmetic  1.84 us (1%)
  between operations  1.48 us (1%)
    pallas_call x1, Pallas kernels, project(): pl.pallas_call(functools.partial(project_kernel, cfg), in_specs=[vmem] *...  53.6 us
    pallas_call x1, Pallas kernels, finish(): pl.pallas_call(functools.partial(finish_kernel, cfg), in_specs=[hbm, hbm,...  50.9 us
    pallas_call x1, Pallas kernels, attend(): pl.pallas_call(functools.partial(attend_kernel, group), grid=(heads,), in...  30.7 us
    unnamed x19, local copies, waits for them, and re-layouts  6.14 us

profile of v2, /device:TPU:0, one launch (start us, length us, event | category | flops | bytes accessed | tf_op | source)
XLA Modules:
  0.0 144.6 jit_solution(1235642739589762256)
XLA Ops:
  0.0 0.8 select_reduce_fusion.holds
  0.8 0.0 copy-start.5
  0.8 0.0 copy-start.6
  0.9 0.0 copy-start.7
  0.9 0.0 copy-start.8
  0.9 0.0 copy-start.2
  0.9 0.0 copy-start.3
  0.9 0.0 copy-start.4
  0.9 3.6 %copy.16 = bf16[128,8,2,512]{3,1,2,0:T(8,128)(2,1)} copy(bf16[128,8,2,512]{3,2,1,0:T(2,128)(2,1)} %bitcast.7) | data formatting | bytes 4194304
  4.5 0.0 copy-done.5
  4.5 0.0 copy-done.6
  4.5 0.0 copy-done.7
  4.5 0.0 copy-done.8
  5.2 0.0 copy-done.2
  5.3 0.0 copy-done.3
  5.3 0.0 copy-done.4
  5.3 53.6 %project.1 = (bf16[8,2,384,128]{3,2,1,0:T(8,128)(2,1)}, bf16[4,1024,512]{2,1,0:T(8,128)(2,1)}, s32[8,8,128]{2,1,0:T(8,128)S(1)}, bf16[2,2,384,128]{3,2,1,0:T(8,128)(2,1)S(1)}, f32[2,8,128]{2,1,0:T(8,128)S(1)}) custom-call(bf16[128,2560]{1,0:T(8,128)(2,1)S(1)} %copy-done.2, f32[8,2560]{1,0:T(8,128)S(1)} %broadcast_in_dim.46.gain, ...), custom_call_target="tpu_custom_call" | custom-call | tf_op jit(solution)/shard_map/project/pallas_call | solution.py:263
  58.9 0.0 copy-start
  58.9 1.4 copy-done
  60.3 30.7 %attend.1 = (bf16[8,2,384,128]{3,2,1,0:T(8,128)(2,1)S(1)}, f32[8,2,8,128]{3,2,1,0:T(8,128)S(1)}) custom-call(s32[4]{0:T(128)S(1)} %select_reduce_fusion.holds, s32[8,8,128]{2,1,0:T(8,128)S(1)} %get-tuple-element.12.prefixes, bf16[8,2,384,128]{3,2,1,0:T(8,128)(2,1)S(1)} %copy-done, bf16[4,1024,512]{2,1,0:T(8,128)(2,1)} %get-tuple-element.14.ks.vs, ...), custom_call_target="tpu_custom_call" | custom-call | tf_op jit(solution)/shard_map/attend/pallas_call | solution.py:343
  90.9 0.0 copy-start.1
  91.0 1.1 copy-done.1
  92.1 50.9 %finish.1 = f32[128,2560]{1,0:T(8,128)S(1)} custom-call(bf16[8,2,384,128]{3,2,1,0:T(8,128)(2,1)} %copy-done.1, f32[8,2,8,128]{3,2,1,0:T(8,128)S(1)} %get-tuple-element.16.lses, bf16[2,2,384,128]{3,2,1,0:T(8,128)(2,1)S(1)} %get-tuple-element.17.own_out, f32[2,8,128]{2,1,0:T(8,128)S(1)} %get-tuple-element.18.own_lse, bf16[1536,5120]{1,0:T(8,128)(2,1)} %wo.1), custom_call_target="tpu_custom_call" | custom-call | tf_op jit(solution)/shard_map/finish/pallas_call | solution.py:511
  143.6 1.0 select_convert_fusion
  (9 shorter events, 0.1 us)
Async XLA Ops:
  0.8 3.6 %copy-start.5 = (bf16[2560]{0:T(1024)(128)(2,1)S(1)}, bf16[2560]{0:T(1024)(128)(2,1)}, u32[]{:S(2)}) copy-start(bf16[2560]{0:T(1024)(128)(2,1)} %param.16) | copy-start | bytes 15364
  0.8 3.6 %copy-start.6 = (bf16[1536]{0:T(1024)(128)(2,1)S(1)}, bf16[1536]{0:T(1024)(128)(2,1)}, u32[]{:S(2)}) copy-start(bf16[1536]{0:T(1024)(128)(2,1)} %param.18) | copy-start | bytes 9220
  0.9 3.7 %copy-start.7 = (bf16[512]{0:T(512)(128)(2,1)S(1)}, bf16[512]{0:T(512)(128)(2,1)}, u32[]{:S(2)}) copy-start(bf16[512]{0:T(512)(128)(2,1)} %param.20) | copy-start | bytes 3076
  0.9 3.7 %copy-start.8 = (bf16[512]{0:T(512)(128)(2,1)S(1)}, bf16[512]{0:T(512)(128)(2,1)}, u32[]{:S(2)}) copy-start(bf16[512]{0:T(512)(128)(2,1)} %param.22) | copy-start | bytes 3076
  0.9 4.4 %copy-start.2 = (bf16[128,2560]{1,0:T(8,128)(2,1)S(1)}, bf16[128,2560]{1,0:T(8,128)(2,1)}, u32[]{:S(2)}) copy-start(bf16[128,2560]{1,0:T(8,128)(2,1)} %hidden.1) | copy-start | bytes 1966084
  0.9 4.4 %copy-start.3 = (f32[128,128]{1,0:T(8,128)S(1)}, f32[128,128]{1,0:T(8,128)}, u32[]{:S(2)}) copy-start(f32[128,128]{1,0:T(8,128)} %constant.50.clone.cosine) | copy-start | bytes 196612
  0.9 4.4 %copy-start.4 = (f32[128,128]{1,0:T(8,128)S(1)}, f32[128,128]{1,0:T(8,128)}, u32[]{:S(2)}) copy-start(f32[128,128]{1,0:T(8,128)} %constant.51.clone.sine) | copy-start | bytes 196612
  58.9 1.4 copy-start
  90.9 1.1 copy-start.1

commit v3 on v2

--- a/solution.py
+++ b/solution.py
@@ -11,7 +11,7 @@
 HD = 128
 NPREF = 4
 OUTER = 4
-PIECES = 2
+PIECES = 4
 PAD = 8
 
 THETA = 1000000.0
@@ -299,16 +299,17 @@
     )(hidden, gain, bias, cosine, sine, prefix, kvs, wq, wk, wv)
 
 
-def attend_kernel(group, holds, prefixes, qs, ks, vs, out, lse, ones, acc, peak):
+def attend_kernel(group, holds, prefixes, qs, ks, vs, out, lse, acc, peak, total):
     slots, _, rows, _ = qs.shape
     inner, block, _ = ks.shape
     length = rows // group
     scale = HD ** (-0.5)
     base2 = scale * np.log2(np.e)
     peak[...] = jnp.full_like(peak, LOWEST)
+    total[...] = jnp.zeros_like(total)
     acc[...] = jnp.zeros_like(acc)
-    ones[:, :, :HD] = vs[...]
-    ones[:, :, HD:] = jnp.ones((inner, block, HD), jnp.bfloat16)
+    part = rows // 2
+    halves = [slice(n * part, (n + 1) * part) for n in range(2)]
 
     @pl.loop(0, slots * inner)
     def _(pair):
@@ -316,24 +317,29 @@
 
         @pl.when(prefixes[s, 0, 0] == holds[k])
         def _():
-            scores = lax.dot_general(qs[s, 0], ks[k], NT, preferred_element_type=jnp.float32)
-            old = peak[s]
-            top = jnp.maximum(old, jnp.max(scores, axis=1, keepdims=True))
-            weights = jnp.exp2((scores - top) * base2)
-            fade = jnp.exp2((old - top) * base2)
-            peak[s] = top
-            acc[s] = acc[s] * fade + jnp.dot(
-                weights.astype(jnp.bfloat16), ones[k], preferred_element_type=jnp.float32
-            )
+            both = [
+                lax.dot_general(qs[s, 0, at], ks[k], NT, preferred_element_type=jnp.float32)
+                for at in halves
+            ]
+            for at, scores in zip(halves, both):
+                old = peak[s, at]
+                top = jnp.maximum(old, jnp.max(scores, axis=1, keepdims=True))
+                weights = jnp.exp2((scores - top) * base2)
+                fade = jnp.exp2((old - top) * base2)
+                peak[s, at] = top
+                total[s, at] = total[s, at] * fade + jnp.sum(weights, axis=1, keepdims=True)
+                acc[s, at] = acc[s, at] * fade + jnp.dot(
+                    weights.astype(jnp.bfloat16), vs[k], preferred_element_type=jnp.float32
+                )
 
     @pl.loop(0, slots)
     def _(s):
-        whole = acc[s, :, HD:]
-        some = whole > 0.0
-        safe = jnp.where(some, whole, 1.0)
-        out[s, 0] = (acc[s, :, :HD] / safe).astype(jnp.bfloat16)
-        column = jnp.where(some[:, :1], peak[s] * scale + jnp.log(safe[:, :1]), LOWEST)
-        lse[s, 0] = to_row(heads_of(column, group, length), length)
+        whole = total[s]
+        out[s, 0] = (acc[s] * (1.0 / jnp.where(whole > 0.0, whole, 1.0))).astype(jnp.bfloat16)
+        tops = to_row(heads_of(peak[s], group, length), length)
+        sums = to_row(heads_of(whole, group, length), length)
+        some = sums > 0.0
+        lse[s, 0] = jnp.where(some, tops * scale + jnp.log(jnp.where(some, sums, 1.0)), LOWEST)
 
 
 def attend(holds, prefixes, qg, kvg, group):
@@ -355,15 +361,15 @@
             pl.BlockSpec((slots, 1, PAD, length), lambda g: (0, g, 0, 0)),
         ],
         scratch_shapes=[
-            pltpu.VMEM((inner, block, 2 * HD), jnp.bfloat16),
-            pltpu.VMEM((slots, rows, 2 * HD), jnp.float32),
+            pltpu.VMEM((slots, rows, HD), jnp.float32),
+            pltpu.VMEM((slots, rows, 1), jnp.float32),
             pltpu.VMEM((slots, rows, 1), jnp.float32),
         ],
         out_shape=[
             jax.ShapeDtypeStruct((slots, heads, rows, HD), jnp.bfloat16),
             jax.ShapeDtypeStruct((slots, heads, PAD, length), jnp.float32),
         ],
-        compiler_params=pltpu.CompilerParams(vmem_limit_bytes=48 * MIB),
+        compiler_params=pltpu.CompilerParams(vmem_limit_bytes=60 * MIB),
         name="attend",
     )(holds, prefixes, qg, kvg, kvg)
 

time: 145 us -> 137 us (0.945)
  Pallas kernels: 135 us -> 128 us
    pallas_call x1, Pallas kernels: 30.7 us -> 24.7 us  [attend(): pl.pallas_call(functools.partial(attend_kernel, group), grid=(heads,), in...]
where the time goes in v3:
time: 137 us
  Pallas kernels  128 us (93%)
  local copies, waits for them, and re-layouts  5.06 us (4%)
  other arithmetic  2.43 us (2%)
  between operations  1.44 us (1%)
    pallas_call x1, Pallas kernels, project(): pl.pallas_call(functools.partial(project_kernel, cfg), in_specs=[vmem] *...  54.1 us
    pallas_call x1, Pallas kernels, finish(): pl.pallas_call(functools.partial(finish_kernel, cfg), in_specs=[hbm, hbm,...  49.4 us
    pallas_call x1, Pallas kernels, attend(): pl.pallas_call(functools.partial(attend_kernel, group), grid=(heads,), in...  24.7 us
    unnamed x19, local copies, waits for them, and re-layouts  5.04 us

profile of v3, /device:TPU:0, one launch (start us, length us, event | category | flops | bytes accessed | tf_op | source)
XLA Modules:
  0.0 137.1 jit_solution(2556134364676247833)
XLA Ops:
  0.0 1.4 %select_reduce_fusion.holds = s32[4]{0:T(128)} fusion(s32[16]{0:T(128)S(1)} %and_select_fusion, s32[16]{0:T(128)} %param.27, s32[4]{0:T(128)S(1)} %xor_add_fusion), kind=kLoop, calls=%fused_computation.2 | loop fusion | flops 188 | bytes 160 | tf_op jit(solution)/shard_map/reduce_sum | solution.py:576
  1.4 0.0 copy-start.5
  1.4 0.0 copy-start.6
  1.4 0.0 copy-start.7
  1.4 0.0 copy-start.8
  1.4 0.0 copy-start
  1.5 0.0 copy-start.1
  1.5 0.0 copy-start.2
  1.5 3.6 %copy.16 = bf16[128,8,2,512]{3,1,2,0:T(8,128)(2,1)} copy(bf16[128,8,2,512]{3,2,1,0:T(2,128)(2,1)} %bitcast.7) | data formatting | bytes 4194304
  5.0 0.0 copy-done.5
  5.0 0.0 copy-done.6
  5.1 0.0 copy-done.7
  5.1 0.0 copy-done.8
  5.8 0.0 copy-done
  5.8 0.0 copy-done.1
  5.8 0.0 copy-done.2
  5.8 54.1 %project.1 = (bf16[8,2,384,128]{3,2,1,0:T(8,128)(2,1)}, bf16[4,1024,512]{2,1,0:T(8,128)(2,1)}, s32[8,8,128]{2,1,0:T(8,128)S(1)}, bf16[2,2,384,128]{3,2,1,0:T(8,128)(2,1)S(1)}, f32[2,8,128]{2,1,0:T(8,128)S(1)}) custom-call(bf16[128,2560]{1,0:T(8,128)(2,1)S(1)} %copy-done, f32[8,2560]{1,0:T(8,128)S(1)} %broadcast_in_dim.46.gain, ...), custom_call_target="tpu_custom_call" | custom-call | tf_op jit(solution)/shard_map/project/pallas_call | solution.py:263
  59.9 0.0 copy-start.4
  59.9 0.6 copy-done.4
  60.5 24.7 %attend.1 = (bf16[8,2,384,128]{3,2,1,0:T(8,128)(2,1)}, f32[8,2,8,128]{3,2,1,0:T(8,128)}) custom-call(s32[4]{0:T(128)} %select_reduce_fusion.holds, s32[8,8,128]{2,1,0:T(8,128)} %copy-done.4, bf16[8,2,384,128]{3,2,1,0:T(8,128)(2,1)} %get-tuple-element.13.qs, bf16[4,1024,512]{2,1,0:T(8,128)(2,1)} %get-tuple-element.14.ks.vs, ...), custom_call_target="tpu_custom_call" | custom-call | tf_op jit(solution)/shard_map/attend/pallas_call | solution.py:349
  85.2 0.0 copy-start.3
  85.2 0.8 copy-done.3
  86.1 49.4 %finish.1 = f32[128,2560]{1,0:T(8,128)S(1)} custom-call(bf16[8,2,384,128]{3,2,1,0:T(8,128)(2,1)} %get-tuple-element.15.outs, f32[8,2,8,128]{3,2,1,0:T(8,128)S(1)} %copy-done.3, bf16[2,2,384,128]{3,2,1,0:T(8,128)(2,1)S(1)} %get-tuple-element.17.own_out, f32[2,8,128]{2,1,0:T(8,128)S(1)} %get-tuple-element.18.own_lse, bf16[1536,5120]{1,0:T(8,128)(2,1)} %wo.1), custom_call_target="tpu_custom_call" | custom-call | tf_op jit(solution)/shard_map/finish/pallas_call | solution.py:517
  136.2 1.0 select_convert_fusion
  (9 shorter events, 0.1 us)
Async XLA Ops:
  1.4 3.6 %copy-start.5 = (bf16[2560]{0:T(1024)(128)(2,1)S(1)}, bf16[2560]{0:T(1024)(128)(2,1)}, u32[]{:S(2)}) copy-start(bf16[2560]{0:T(1024)(128)(2,1)} %param.16) | copy-start | bytes 15364
  1.4 3.6 %copy-start.6 = (bf16[1536]{0:T(1024)(128)(2,1)S(1)}, bf16[1536]{0:T(1024)(128)(2,1)}, u32[]{:S(2)}) copy-start(bf16[1536]{0:T(1024)(128)(2,1)} %param.18) | copy-start | bytes 9220
  1.4 3.6 %copy-start.7 = (bf16[512]{0:T(512)(128)(2,1)S(1)}, bf16[512]{0:T(512)(128)(2,1)}, u32[]{:S(2)}) copy-start(bf16[512]{0:T(512)(128)(2,1)} %param.20) | copy-start | bytes 3076
  1.4 3.7 %copy-start.8 = (bf16[512]{0:T(512)(128)(2,1)S(1)}, bf16[512]{0:T(512)(128)(2,1)}, u32[]{:S(2)}) copy-start(bf16[512]{0:T(512)(128)(2,1)} %param.22) | copy-start | bytes 3076
  1.4 4.4 %copy-start = (bf16[128,2560]{1,0:T(8,128)(2,1)S(1)}, bf16[128,2560]{1,0:T(8,128)(2,1)}, u32[]{:S(2)}) copy-start(bf16[128,2560]{1,0:T(8,128)(2,1)} %hidden.1) | copy-start | bytes 1966084
  1.5 4.4 %copy-start.1 = (f32[128,128]{1,0:T(8,128)S(1)}, f32[128,128]{1,0:T(8,128)}, u32[]{:S(2)}) copy-start(f32[128,128]{1,0:T(8,128)} %constant.50.clone.cosine) | copy-start | bytes 196612
  1.5 4.4 %copy-start.2 = (f32[128,128]{1,0:T(8,128)S(1)}, f32[128,128]{1,0:T(8,128)}, u32[]{:S(2)}) copy-start(f32[128,128]{1,0:T(8,128)} %constant.51.clone.sine) | copy-start | bytes 196612
  59.9 0.6 copy-start.4
  85.2 0.8 copy-start.3
